TPU v7x, 128 devices: a whole 4x4x4 slice. The times are simulated.
128 devices in a mesh: blk: 16 (over z, y), tok: 8 (over x, core).
Axes of the slice: x: 4, y: 4, z: 4, core: 2. Of those that a mesh axis runs over, the one named last changes fastest.
Arguments:
- inputs: bfloat16 [2048, 8, 2048], P('blk', 'tok'), may hold values from -6 to 6
- resets: int32 [2048, 8], P(None, 'tok'), may hold values from 0 to 1, as said below
- gain_rec: float32 [2048], replicated, may hold values from 0.5 to 1.5
- w_branch: bfloat16 [2048, 2560], P('tok', 'blk'), may hold values from -0.125 to 0.125
- w_gelu: bfloat16 [2048, 2560], P('tok', 'blk'), may hold values from -0.125 to 0.125
- conv_weight: float32 [4, 2560], P(None, 'blk'), may hold values from -3 to 3
- conv_bias: float32 [2560], P('blk'), may hold values from -1.5 to 1.5
- gate_a_weight: bfloat16 [16, 160, 160], P('blk'), may hold values from -0.5 to 0.5
- gate_a_bias: float32 [2560], P('blk'), may hold values from -2.5 to 2.5
- gate_x_weight: bfloat16 [16, 160, 160], P('blk'), may hold values from -0.5 to 0.5
- gate_x_bias: float32 [2560], P('blk'), may hold values from -2.5 to 2.5
- decay_param: float32 [2560], P('blk'), may hold values from 3.5 to 9
- w_out: bfloat16 [2048, 2560], P('tok', 'blk'), may hold values from -0.3125 to 0.3125
- gain_mlp: float32 [2048], replicated, may hold values from 0.5 to 1.5
- w_gate: bfloat16 [2048, 6144], P('tok', 'blk'), may hold values from -0.125 to 0.125
- w_up: bfloat16 [2048, 6144], P('tok', 'blk'), may hold values from -0.125 to 0.125
- w_down: bfloat16 [2048, 6144], P('tok', 'blk'), may hold values from -0.15625 to 0.15625
- cotangent: bfloat16 [2048, 8, 2048], P('blk', 'tok'), may hold values from -6 to 6
Outputs:
- output: bfloat16 [2048, 8, 2048], P('blk', 'tok')
- grad_inputs: float32 [2048, 8, 2048], P('blk', 'tok')
- grad_gain_rec: float32 [2048], replicated
- grad_w_branch: float32 [2048, 2560], P('tok', 'blk')
- grad_w_gelu: float32 [2048, 2560], P('tok', 'blk')
- grad_conv_weight: float32 [4, 2560], P(None, 'blk')
- grad_conv_bias: float32 [2560], P('blk')
- grad_gate_a_weight: float32 [16, 160, 160], P('blk')
- grad_gate_a_bias: float32 [2560], P('blk')
- grad_gate_x_weight: float32 [16, 160, 160], P('blk')
- grad_gate_x_bias: float32 [2560], P('blk')
- grad_decay_param: float32 [2560], P('blk')
- grad_w_out: float32 [2048, 2560], P('tok', 'blk')
- grad_gain_mlp: float32 [2048], replicated
- grad_w_gate: float32 [2048, 6144], P('tok', 'blk')
- grad_w_up: float32 [2048, 6144], P('tok', 'blk')
- grad_w_down: float32 [2048, 6144], P('tok', 'blk')
Inputs may be any that keep to these rules, and one draw needn't show every extreme that they name: `resets`: position 0 of every sequence is 1. Among the 1 sequence held by one index of tok, one has no 1 at positions 128 to 1919.
All inputs are finite; a program needn't handle non-finite values.
Results may differ from a plain program's by a relative error of at most 0.028.
Values may be sent and summed in bfloat16 or wider, within the bound.
A program may use at most 256 MiB of HBM per device.

v0:
```python
import math

import jax
import jax.numpy as jnp
from jax import lax
from jax.sharding import PartitionSpec as P

EPSILON = 1e-06


def scattered(contribution, rows, axis):
    whole = contribution(jnp.int32(0), rows * lax.axis_size(axis)).astype(jnp.bfloat16)
    return lax.psum_scatter(whole, axis, scatter_dimension=0, tiled=True).astype(jnp.float32)


def rms_scale(values, gain_vector):
    return (
        values
        * lax.rsqrt(jnp.mean(values * values, axis=-1, keepdims=True) + EPSILON)
        * gain_vector
    )


def causal_conv(branch, conv_weight, conv_bias, document):
    length = branch.shape[0]
    total = conv_bias + conv_weight[0] * branch
    for offset in range(1, conv_weight.shape[0]):
        moved = jnp.pad(branch[: length - offset], ((offset, 0), (0, 0), (0, 0)))
        moved_doc = jnp.pad(document[: length - offset], ((offset, 0), (0, 0)), constant_values=-1)
        same_doc = (moved_doc == document).astype(branch.dtype)[:, :, None]
        total = total + conv_weight[offset] * moved * same_doc
    return total


def split_blocks(values, blocks):
    length, seq_count, channels = values.shape
    return values.reshape(length, seq_count, blocks, channels // blocks)


def block_mix(values, weight):
    split_up = split_blocks(values, weight.shape[0])
    mixed_out = jnp.einsum("lshi,hij->lshj", split_up, weight, preferred_element_type=jnp.float32)
    return mixed_out.reshape(values.shape)


def block_back(grads_low, weight):
    split_up = split_blocks(grads_low, weight.shape[0])
    mixed_out = jnp.einsum("lshj,hij->lshi", split_up, weight, preferred_element_type=jnp.float32)
    return mixed_out.reshape(grads_low.shape)


def block_grad(values, grads_low, blocks):
    return jnp.einsum(
        "lshi,lshj->hij",
        split_blocks(values, blocks),
        split_blocks(grads_low, blocks),
        preferred_element_type=jnp.float32,
    )


def linear_scan(decay_rate, driven):
    length, seq_count, channels = decay_rate.shape
    piece = math.gcd(length, 16)
    count = length // piece
    rates = decay_rate.reshape(count, piece, seq_count, channels)
    drives = driven.reshape(count, piece, seq_count, channels)
    running = drives[:, 0]
    product = rates[:, 0]
    locals_list = [running]
    products_list = [product]
    for step in range(1, piece):
        running = rates[:, step] * running + drives[:, step]
        product = product * rates[:, step]
        locals_list.append(running)
        products_list.append(product)

    def combine(earlier, later):
        return (earlier[0] * later[0], later[0] * earlier[1] + later[1])

    inclusive = lax.associative_scan(combine, (product, running), axis=0)[1]
    entering = jnp.concatenate([jnp.zeros_like(inclusive[:1]), inclusive[:-1]], axis=0)
    local_states = jnp.stack(locals_list, axis=1)
    local_products = jnp.stack(products_list, axis=1)
    states = local_states + local_products * entering[:, None]
    return states.reshape(length, seq_count, channels)


def recurrence(conv_out, pre_rate, pre_admit, rate_bias, admit_bias, decay_param, resets):
    rate_gate = jax.nn.sigmoid(pre_rate + rate_bias)
    admit_gate = jax.nn.sigmoid(pre_admit + admit_bias)
    log_decay = -8.0 * rate_gate * jax.nn.softplus(-decay_param)
    restart = (resets == 1)[:, :, None]
    decay_rate = jnp.where(restart, 0.0, jnp.exp(log_decay))
    scaling = jnp.where(restart, 1.0, jnp.sqrt(-jnp.expm1(2.0 * log_decay)))
    driven = scaling * admit_gate * conv_out
    return linear_scan(decay_rate, driven)


def matmul(left, right):
    return jnp.dot(left, right, preferred_element_type=jnp.float32)


def matmul_back(left, right):
    return lax.dot_general(
        left, right, (((1,), (1,)), ((), ())), preferred_element_type=jnp.float32
    )


def matmul_rows(left, right):
    return lax.dot_general(
        left, right, (((0,), (0,)), ((), ())), preferred_element_type=jnp.float32
    )


def on_device(
    inputs,
    resets,
    gain_rec,
    w_branch,
    w_gelu,
    conv_weight,
    conv_bias,
    gate_a_weight,
    gate_a_bias,
    gate_x_weight,
    gate_x_bias,
    decay_param,
    w_out,
    gain_mlp,
    w_gate,
    w_up,
    w_down,
    cotangent,
):
    shard_len, seq_count, model_width = inputs.shape
    row_count = shard_len * seq_count
    flat = inputs.reshape(row_count, model_width).astype(jnp.float32)
    full_branch, full_gelu, full_out, full_gate, full_up, full_down = (
        lax.all_gather(w_branch, "tok", axis=0, tiled=True),
        lax.all_gather(w_gelu, "tok", axis=0, tiled=True),
        lax.all_gather(w_out, "tok", axis=0, tiled=True),
        lax.all_gather(w_gate, "tok", axis=0, tiled=True),
        lax.all_gather(w_up, "tok", axis=0, tiled=True),
        lax.all_gather(w_down, "tok", axis=0, tiled=True),
    )
    normed, norm_rec_back = jax.vjp(rms_scale, flat, gain_rec)
    normed_low = normed.astype(jnp.bfloat16)
    seq_normed = lax.all_gather(normed_low, "blk", axis=0, tiled=True)
    length = seq_normed.shape[0] // seq_count
    channels = full_branch.shape[1]
    document = jnp.cumsum(resets, axis=0)
    branch = matmul(seq_normed, full_branch).reshape(length, seq_count, channels)
    gelu_pre = matmul(seq_normed, full_gelu)
    conv_out, conv_back = jax.vjp(
        lambda source, weight, shift_bias: causal_conv(source, weight, shift_bias, document),
        branch,
        conv_weight,
        conv_bias,
    )
    conv_low = conv_out.astype(jnp.bfloat16)
    pre_rate = block_mix(conv_low, gate_a_weight)
    pre_admit = block_mix(conv_low, gate_x_weight)
    states, state_back = jax.vjp(
        lambda driver, rate_in, admit_in, rate_bias, admit_bias, decay_in: recurrence(
            driver, rate_in, admit_in, rate_bias, admit_bias, decay_in, resets
        ),
        conv_out,
        pre_rate,
        pre_admit,
        gate_a_bias,
        gate_x_bias,
        decay_param,
    )
    states_flat = states.reshape(length * seq_count, channels)
    gelu_out, gelu_back = jax.vjp(jax.nn.gelu, gelu_pre)
    gated = (states_flat * gelu_out).astype(jnp.bfloat16)
    rec_out = scattered(
        lambda row_start, row_number: matmul_back(gated, full_out), row_count, "blk"
    )
    mixed_rows = flat + rec_out
    normed_mlp, norm_mlp_back = jax.vjp(rms_scale, mixed_rows, gain_mlp)
    mlp_low = normed_mlp.astype(jnp.bfloat16)
    seq_mlp = lax.all_gather(mlp_low, "blk", axis=0, tiled=True)
    gate_pre = matmul(seq_mlp, full_gate)
    up_pre = matmul(seq_mlp, full_up)
    hidden, hidden_back = jax.vjp(lambda left, right: jax.nn.gelu(left) * right, gate_pre, up_pre)
    hidden_low = hidden.astype(jnp.bfloat16)
    mlp_out = scattered(
        lambda row_start, row_number: matmul_back(hidden_low, full_down), row_count, "blk"
    )
    output = (mixed_rows + mlp_out).astype(jnp.bfloat16).reshape(shard_len, seq_count, model_width)
    grad_out = cotangent.reshape(row_count, model_width)
    seq_grad = lax.all_gather(grad_out, "blk", axis=0, tiled=True)
    grad_w_down = matmul_rows(seq_grad, hidden_low)
    grad_hidden = matmul(seq_grad, full_down)
    grad_gate, grad_up = hidden_back(grad_hidden)
    gate_low = grad_gate.astype(jnp.bfloat16)
    up_low = grad_up.astype(jnp.bfloat16)
    grad_w_gate = matmul_rows(seq_mlp, gate_low)
    grad_w_up = matmul_rows(seq_mlp, up_low)
    back_mlp = scattered(
        lambda row_start, row_number: matmul_back(gate_low, full_gate)
        + matmul_back(up_low, full_up),
        row_count,
        "blk",
    )
    grad_mixed_norm, grad_gain_mlp = norm_mlp_back(back_mlp)
    grad_mixed = grad_out.astype(jnp.float32) + grad_mixed_norm
    seq_mixed = lax.all_gather(grad_mixed.astype(jnp.bfloat16), "blk", axis=0, tiled=True)
    grad_w_out = matmul_rows(seq_mixed, gated)
    grad_gated = matmul(seq_mixed, full_out)
    grad_states = grad_gated * gelu_out
    (grad_gelu_pre,) = gelu_back(grad_gated * states_flat)
    gelu_low = grad_gelu_pre.astype(jnp.bfloat16)
    grad_conv, grad_rate, grad_admit, grad_rate_bias, grad_admit_bias, grad_decay = state_back(
        grad_states.reshape(length, seq_count, channels)
    )
    rate_low = grad_rate.astype(jnp.bfloat16)
    admit_low = grad_admit.astype(jnp.bfloat16)
    blocks = gate_a_weight.shape[0]
    grad_gate_a = block_grad(conv_low, rate_low, blocks)
    grad_gate_x = block_grad(conv_low, admit_low, blocks)
    grad_conv = (
        grad_conv + block_back(rate_low, gate_a_weight) + block_back(admit_low, gate_x_weight)
    )
    grad_branch, grad_conv_weight, grad_conv_bias = conv_back(grad_conv)
    branch_low = grad_branch.reshape(length * seq_count, channels).astype(jnp.bfloat16)
    grad_w_branch = matmul_rows(seq_normed, branch_low)
    grad_w_gelu = matmul_rows(seq_normed, gelu_low)
    back_rec = scattered(
        lambda row_start, row_number: matmul_back(branch_low, full_branch)
        + matmul_back(gelu_low, full_gelu),
        row_count,
        "blk",
    )
    grad_flat, grad_gain_rec = norm_rec_back(back_rec)
    grad_inputs = (grad_mixed + grad_flat).reshape(shard_len, seq_count, model_width)
    small_sums = (
        lax.psum(grad_conv_weight.astype(jnp.bfloat16), "tok").astype(jnp.float32),
        lax.psum(grad_conv_bias.astype(jnp.bfloat16), "tok").astype(jnp.float32),
        lax.psum(grad_gate_a.astype(jnp.bfloat16), "tok").astype(jnp.float32),
        lax.psum(grad_rate_bias.astype(jnp.bfloat16), "tok").astype(jnp.float32),
        lax.psum(grad_gate_x.astype(jnp.bfloat16), "tok").astype(jnp.float32),
        lax.psum(grad_admit_bias.astype(jnp.bfloat16), "tok").astype(jnp.float32),
        lax.psum(grad_decay.astype(jnp.bfloat16), "tok").astype(jnp.float32),
    )
    gain_sums = lax.psum((grad_gain_rec, grad_gain_mlp), ("blk", "tok"))
    shards = (
        lax.psum_scatter(
            grad_w_branch.astype(jnp.bfloat16), "tok", scatter_dimension=0, tiled=True
        ).astype(jnp.float32),
        lax.psum_scatter(
            grad_w_gelu.astype(jnp.bfloat16), "tok", scatter_dimension=0, tiled=True
        ).astype(jnp.float32),
        lax.psum_scatter(
            grad_w_out.astype(jnp.bfloat16), "tok", scatter_dimension=0, tiled=True
        ).astype(jnp.float32),
        lax.psum_scatter(
            grad_w_gate.astype(jnp.bfloat16), "tok", scatter_dimension=0, tiled=True
        ).astype(jnp.float32),
        lax.psum_scatter(
            grad_w_up.astype(jnp.bfloat16), "tok", scatter_dimension=0, tiled=True
        ).astype(jnp.float32),
        lax.psum_scatter(
            grad_w_down.astype(jnp.bfloat16), "tok", scatter_dimension=0, tiled=True
        ).astype(jnp.float32),
    )
    return (
        output,
        grad_inputs,
        gain_sums[0],
        shards[0],
        shards[1],
        small_sums[0],
        small_sums[1],
        small_sums[2],
        small_sums[3],
        small_sums[4],
        small_sums[5],
        small_sums[6],
        shards[2],
        gain_sums[1],
        shards[3],
        shards[4],
        shards[5],
    )


def solution(mesh):
    in_specs = (
        P("blk", "tok", None),
        P(None, "tok"),
        P(),
        P("tok", "blk"),
        P("tok", "blk"),
        P(None, "blk"),
        P("blk"),
        P("blk", None, None),
        P("blk"),
        P("blk", None, None),
        P("blk"),
        P("blk"),
        P("tok", "blk"),
        P(),
        P("tok", "blk"),
        P("tok", "blk"),
        P("tok", "blk"),
        P("blk", "tok", None),
    )
    out_specs = (
        P("blk", "tok", None),
        P("blk", "tok", None),
        P(),
        P("tok", "blk"),
        P("tok", "blk"),
        P(None, "blk"),
        P("blk"),
        P("blk", None, None),
        P("blk"),
        P("blk", None, None),
        P("blk"),
        P("blk"),
        P("tok", "blk"),
        P(),
        P("tok", "blk"),
        P("tok", "blk"),
        P("tok", "blk"),
    )
    return jax.shard_map(
        on_device, mesh=mesh, in_specs=in_specs, out_specs=out_specs, check_vma=False
    )
```

profile of v0, /device:TPU:1, one launch (start us, length us, event | category | flops | bytes accessed | tf_op | source)
XLA Modules:
  0.0 1591.2 jit_solution(12480051463898608941)
XLA Ops:
  13.1 14.9 all_gather.31
  57.0 28.8 %all-gather.9.cloned.1.call-done = bf16[2048,2048]{1,0:T(8,128)(2,1)} async-done(((bf16[128,2048]{1,0:T(8,128)(2,1)}), bf16[2048,2048]{1,0:T(8,128)(2,1)}) %all-gather.9.cloned.1.call-update) | async-done | bytes 8388624 | tf_op jit(solution)/shard_map/all_gather | solution.py:148
  151.4 28.1 %pad.616 = f32[127,1,160]{2,1,0:T(1,128)} pad(f32[64,1,160]{2,1,0:T(1,128)} %pad_maximum_fusion, f32[]{:T(128)} %constant.19.clone.1), padding=0_0_1x0_0_0x0_0_0 | pad | bytes 122244 | tf_op jit(solution)/shard_map/jvp()/slice | solution.py:81
  179.6 27.3 %pad.761 = f32[128,1,160]{2,1,0:T(1,128)} pad(f32[64,1,160]{2,1,0:T(1,128)} %add.1595, f32[]{:T(128)} %constant.19.clone.1), padding=1_0_1x0_0_0x0_0_0 | pad | bytes 122884
  240.4 83.3 %reduce-scatter.11.cloned.1.call-done = bf16[128,2048]{1,0:T(8,128)(2,1)} async-done(((bf16[2048,2048]{1,0:T(8,128)(2,1)}), bf16[128,2048]{1,0:T(8,128)(2,1)}) %reduce-scatter.11.cloned.1.call-update) | async-done | bytes 524304 | tf_op jit(solution)/shard_map/reduce_scatter | solution.py:13
  329.5 69.0 %all-gather.11.cloned.1.call-done = bf16[2048,2048]{1,0:T(8,128)(2,1)} async-done(((bf16[128,2048]{1,0:T(8,128)(2,1)}), bf16[2048,2048]{1,0:T(8,128)(2,1)}) %all-gather.11.cloned.1.call-update) | async-done | bytes 8388624 | tf_op jit(solution)/shard_map/all_gather | solution.py:183
  408.6 15.8 all-gather.13.cloned.1.call-done
  434.4 16.2 %all-gather.17.cloned.1.call-done = bf16[2048,384]{1,0:T(8,128)(2,1)} async-done(((bf16[256,384]{1,0:T(8,128)(2,1)}), bf16[2048,384]{1,0:T(8,128)(2,1)}) %all-gather.17.cloned.1.call-update) | async-done | bytes 1572880 | tf_op jit(solution)/shard_map/all_gather | solution.py:144
  450.6 72.8 %all-gather.21.cloned.1.call-done = bf16[2048,1,2048]{2,0,1:T(8,128)(2,1)} async-done(((bf16[128,1,2048]{2,0,1:T(8,128)(2,1)}), bf16[2048,1,2048]{2,0,1:T(8,128)(2,1)}) %all-gather.21.cloned.1.call-update) | async-done | bytes 8388624 | tf_op jit(solution)/shard_map/all_gather | solution.py:193
  556.1 83.9 %reduce-scatter.15.cloned.1.call-done = bf16[128,2048]{1,0:T(8,128)(2,1)} async-done(((bf16[2048,2048]{1,0:T(8,128)(2,1)}), bf16[128,2048]{1,0:T(8,128)(2,1)}) %reduce-scatter.15.cloned.1.call-update) | async-done | bytes 524304 | tf_op jit(solution)/shard_map/reduce_scatter | solution.py:13
  672.6 42.3 %all-gather.19.cloned.1.call-done = bf16[2048,2048]{1,0:T(8,128)(2,1)} async-done(((bf16[128,2048]{1,0:T(8,128)(2,1)}), bf16[2048,2048]{1,0:T(8,128)(2,1)}) %all-gather.19.cloned.1.call-update) | async-done | bytes 8388624 | tf_op jit(solution)/shard_map/all_gather | solution.py:209
  872.3 14.6 pad.556
  946.6 19.1 %pad.523 = f32[128,1,160]{2,1,0:T(1,128)} pad(f32[64,1,160]{2,1,0:T(1,128)S(1)} %get-tuple-element.159, f32[]{:T(128)} %constant.19.clone.1), padding=1_0_1x0_0_0x0_0_0 | pad | bytes 122884 | tf_op jit(solution)/shard_map/transpose(jvp())/pad | solution.py:80
  965.8 22.1 %pad.558 = f32[128,1,160]{2,1,0:T(1,128)S(1)} pad(f32[64,1,160]{2,1,0:T(1,128)} %get-tuple-element.158, f32[]{:T(128)} %constant.19.clone.1), padding=1_0_1x0_0_0x0_0_0 | pad | bytes 122884 | tf_op jit(solution)/shard_map/transpose(jvp())/pad | solution.py:80
  987.9 28.3 %pad.524 = f32[128,1,160]{2,1,0:T(1,128)} pad(f32[64,1,160]{2,1,0:T(1,128)} %slice_multiply_fusion.27, f32[]{:T(128)} %constant.19.clone.1), padding=0_1_1x0_0_0x0_0_0 | pad | bytes 122884 | tf_op jit(solution)/shard_map/transpose(jvp())/pad | solution.py:80
  1016.1 27.1 %pad.541 = f32[128,1,160]{2,1,0:T(1,128)} pad(f32[63,1,160]{2,1,0:T(1,128)} %get-tuple-element.254, f32[]{:T(128)} %constant.19.clone.1), padding=2_1_1x0_0_0x0_0_0 | pad | bytes 122244 | tf_op jit(solution)/shard_map/transpose(jvp())/pad | solution.py:80
  1043.2 27.6 %pad.559 = f32[128,1,160]{2,1,0:T(1,128)} pad(f32[64,1,160]{2,1,0:T(1,128)} %get-tuple-element.249, f32[]{:T(128)} %constant.19.clone.1), padding=0_1_1x0_0_0x0_0_0 | pad | bytes 122884 | tf_op jit(solution)/shard_map/transpose(jvp())/pad | solution.py:80
  1070.9 27.3 %pad.480 = f32[128,1,160]{2,1,0:T(1,128)} pad(f32[63,1,160]{2,1,0:T(1,128)} %get-tuple-element.256, f32[]{:T(128)} %constant.19.clone.1), padding=2_1_1x0_0_0x0_0_0 | pad | bytes 122244 | tf_op jit(solution)/shard_map/transpose(jvp())/pad | solution.py:80
  1250.3 19.4 %reduce-scatter.23.cloned.1.call-done = bf16[256,160]{0,1:T(8,128)(2,1)} async-done(((bf16[2048,160]{0,1:T(8,128)(2,1)}), bf16[256,160]{0,1:T(8,128)(2,1)}) %reduce-scatter.23.cloned.1.call-update) | async-done | bytes 81936 | tf_op jit(solution)/shard_map/reduce_scatter | solution.py:255
  1271.3 30.9 %reduce-scatter.21.cloned.1.call-done = bf16[256,160]{0,1:T(8,128)(2,1)} async-done(((bf16[2048,160]{0,1:T(8,128)(2,1)}), bf16[256,160]{0,1:T(8,128)(2,1)}) %reduce-scatter.21.cloned.1.call-update) | async-done | bytes 81936 | tf_op jit(solution)/shard_map/reduce_scatter | solution.py:252
  1303.7 31.3 %reduce-scatter.19.cloned.1.call-done = bf16[256,160]{0,1:T(8,128)(2,1)} async-done(((bf16[2048,160]{0,1:T(8,128)(2,1)}), bf16[256,160]{0,1:T(8,128)(2,1)}) %reduce-scatter.19.cloned.1.call-update) | async-done | bytes 81936 | tf_op jit(solution)/shard_map/reduce_scatter | solution.py:249
  1336.6 87.8 %reduce-scatter.17.cloned.1.call-done = bf16[128,2048]{1,0:T(8,128)(2,1)} async-done(((bf16[2048,2048]{1,0:T(8,128)(2,1)}), bf16[128,2048]{1,0:T(8,128)(2,1)}) %reduce-scatter.17.cloned.1.call-update) | async-done | bytes 524304 | tf_op jit(solution)/shard_map/reduce_scatter | solution.py:13
  1426.0 86.9 %reduce-scatter.13.cloned.1.call-done = bf16[128,2048]{1,0:T(8,128)(2,1)} async-done(((bf16[2048,2048]{1,0:T(8,128)(2,1)}), bf16[128,2048]{1,0:T(8,128)(2,1)}) %reduce-scatter.13.cloned.1.call-update) | async-done | bytes 524304 | tf_op jit(solution)/shard_map/reduce_scatter | solution.py:13
  1517.8 65.8 %all-reduce.127 = (f32[2048]{0:T(1024)}, f32[2048]{0:T(1024)}) all-reduce(f32[2048]{0:T(1024)S(1)} %get-tuple-element.87, f32[2048]{0:T(1024)S(1)} %copy-done.149), channel_id=1, replica_groups=mesh['blk'=16,'tok'=8] {'blk','tok'}, use_global_device_ids=true, to_apply=%region_12.13 | all-reduce | flops 4096 | bytes 32768 | tf_op jit(solution)/shard_map/psum | solution.py:247
  (662 shorter events, 602.3 us)
Async XLA Ops:
  8.1 77.7 %all-gather.9.cloned.1.call-start = ((), (), s32[]{:S(2)}) async-start(), calls=%async_computation.10 | async-start | bytes 8912896 | tf_op jit(solution)/shard_map/all_gather | solution.py:148
  11.5 312.2 %reduce-scatter.11.cloned.1.call-start = ((), (), s32[]{:S(2)}) async-start(), calls=%async_computation.11 | async-start | bytes 8912896 | tf_op jit(solution)/shard_map/reduce_scatter | solution.py:13
  239.8 89.6 %all-gather.15.cloned.1.call-start = ((), (), s32[]{:S(2)}) async-start(), calls=%async_computation.14 | async-start | bytes 1769472 | tf_op jit(solution)/shard_map/all_gather | solution.py:143
  240.4 158.1 %all-gather.11.cloned.1.call-start = ((), (), s32[]{:S(2)}) async-start(), calls=%async_computation.12 | async-start | bytes 8912896 | tf_op jit(solution)/shard_map/all_gather | solution.py:183
  325.1 317.1 %copy-start.169 = (f32[128]{0:T(128)}, f32[128]{0:T(128)S(1)}, u32[]{:S(2)}) copy-start(f32[128]{0:T(128)S(1)} %fusion.126) | copy-start | bytes 1540
  327.1 97.3 %all-gather.13.cloned.1.call-start = ((), (), s32[]{:S(2)}) async-start(), calls=%async_computation.13 | async-start | bytes 1769472 | tf_op jit(solution)/shard_map/all_gather | solution.py:142
  327.7 122.9 %all-gather.17.cloned.1.call-start = ((), (), s32[]{:S(2)}) async-start(), calls=%async_computation.15 | async-start | bytes 1769472 | tf_op jit(solution)/shard_map/all_gather | solution.py:144
  328.5 195.0 %all-gather.21.cloned.1.call-start = ((), (), s32[]{:S(2)}) async-start(), calls=%async_computation.26 | async-start | bytes 8912896 | tf_op jit(solution)/shard_map/all_gather | solution.py:193
  329.2 310.8 %reduce-scatter.15.cloned.1.call-start = ((), (), s32[]{:S(2)}) async-start(), calls=%async_computation.17 | async-start | bytes 8912896 | tf_op jit(solution)/shard_map/reduce_scatter | solution.py:13
  556.1 158.9 %all-gather.19.cloned.1.call-start = ((), (), s32[]{:S(2)}) async-start(), calls=%async_computation.18 | async-start | bytes 8912896 | tf_op jit(solution)/shard_map/all_gather | solution.py:209
  643.5 592.3 %reduce-scatter.29.cloned.1.call-start = ((), (), s32[]{:S(2)}) async-start(), calls=%async_computation.25 | async-start | bytes 1769472 | tf_op jit(solution)/shard_map/reduce_scatter | solution.py:264
  652.1 585.5 %reduce-scatter.27.cloned.1.call-start = ((), (), s32[]{:S(2)}) async-start(), calls=%async_computation.24 | async-start | bytes 1769472 | tf_op jit(solution)/shard_map/reduce_scatter | solution.py:261
  662.7 576.7 %reduce-scatter.25.cloned.1.call-start = ((), (), s32[]{:S(2)}) async-start(), calls=%async_computation.23 | async-start | bytes 1769472 | tf_op jit(solution)/shard_map/reduce_scatter | solution.py:258
  672.4 568.8 %all-reduce.131.cloned.1.call-start = ((), (), s32[]{:S(2)}) async-start(), calls=%async_computation.27 | async-start | bytes 335872 | tf_op jit(solution)/shard_map/psum | solution.py:239
  1180.5 89.3 %reduce-scatter.23.cloned.1.call-start = ((), (), s32[]{:S(2)}) async-start(), calls=%async_computation.22 | async-start | bytes 737280 | tf_op jit(solution)/shard_map/reduce_scatter | solution.py:255
  1186.3 115.9 %reduce-scatter.21.cloned.1.call-start = ((), (), s32[]{:S(2)}) async-start(), calls=%async_computation.21 | async-start | bytes 737280 | tf_op jit(solution)/shard_map/reduce_scatter | solution.py:252
  1196.7 138.3 %reduce-scatter.19.cloned.1.call-start = ((), (), s32[]{:S(2)}) async-start(), calls=%async_computation.20 | async-start | bytes 737280 | tf_op jit(solution)/shard_map/reduce_scatter | solution.py:249
  1206.4 218.0 %reduce-scatter.17.cloned.1.call-start = ((), (), s32[]{:S(2)}) async-start(), calls=%async_computation.19 | async-start | bytes 8912896 | tf_op jit(solution)/shard_map/reduce_scatter | solution.py:13
  1226.2 286.7 %reduce-scatter.13.cloned.1.call-start = ((), (), s32[]{:S(2)}) async-start(), calls=%async_computation.16 | async-start | bytes 8912896 | tf_op jit(solution)/shard_map/reduce_scatter | solution.py:13
  1239.3 273.6 %copy-start.32 = (bf16[128,1,2048]{2,0,1:T(8,128)(2,1)S(1)}, bf16[128,1,2048]{2,0,1:T(8,128)(2,1)}, u32[]{:S(2)}) copy-start(bf16[128,1,2048]{2,0,1:T(8,128)(2,1)} %param.35) | copy-start | bytes 1572868
  1239.3 273.6 %copy-start.34 = (bf16[128,2048]{1,0:T(8,128)(2,1)S(1)}, bf16[128,2048]{1,0:T(8,128)(2,1)}, u32[]{:S(2)}) copy-start(bf16[128,2048]{1,0:T(8,128)(2,1)} %reduce-scatter.15.cloned.1.call-done) | copy-start | bytes 1572868
  1239.3 273.6 %copy-start.123 = (f32[2048]{0:T(1024)S(1)}, f32[2048]{0:T(1024)}, u32[]{:S(2)}) copy-start(f32[2048]{0:T(1024)} %param.31) | copy-start | bytes 24580
  1239.3 273.6 %copy-start.170 = (f32[128]{0:T(128)S(1)}, f32[128]{0:T(128)}, u32[]{:S(2)}) copy-start(f32[128]{0:T(128)} %copy-done.169) | copy-start | bytes 1540
  1239.4 273.6 %copy-start.184 = (f32[128]{0:T(128)S(1)}, f32[128]{0:T(128)}, u32[]{:S(2)}) copy-start(f32[128]{0:T(128)} %copy-done.183) | copy-start | bytes 1540
  (185 other events, 2832.3 us)
Sparse Core Ops, SparseCore 0:
  11.7 74.0 all-gather.8
  239.9 83.7 reduce-scatter.10
  556.2 83.7 reduce-scatter.14
Sparse Core Ops, SparseCore 1:
  242.0 24.3 all-gather.14
  327.2 71.2 all-gather.10
  400.0 24.3 all-gather.12
  426.1 24.5 all-gather.16
  452.8 70.6 all-gather.20
  643.6 71.3 all-gather.18
  717.2 29.5 reduce-scatter.28
  749.0 31.4 reduce-scatter.26
  782.7 31.4 reduce-scatter.24
  1180.5 57.3 all-reduce.130
  1240.2 29.4 reduce-scatter.22
  1272.3 29.9 reduce-scatter.20
  1305.1 29.9 reduce-scatter.18
  1338.8 85.5 reduce-scatter.16
  1428.2 84.6 reduce-scatter.12
where the time goes:
time: 1610 us; the launch traced here: 1590 us
  waiting for transfers between devices  671 us (42%)
  local copies, waits for them, and re-layouts  461 us (29%)
  other arithmetic  165 us (10%)
  matrix products  165 us (10%)
  blocking collectives  109 us (7%)
  between operations  18.3 us (1%)
    reduce_scatter x4, waiting for transfers between devices, scattered(): lax.psum_scatter(whole, axis, scatter_dimension=0, tiled=True)  342 us
    pad x50, local copies, waits for them, and re-layouts, linear_scan(): inclusive = lax.associative_scan(combine, (product, running), axis=0)[1]  338 us
    all_gather x1, waiting for transfers between devices, on_device(): seq_grad = lax.all_gather(grad_out, 'blk', axis=0, tiled=True)  72.8 us
    all_gather x1, waiting for transfers between devices, on_device(): seq_mlp = lax.all_gather(mlp_low, 'blk', axis=0, tiled=True)  69 us
    psum x1, blocking collectives, on_device(): gain_sums = lax.psum((grad_gain_rec, grad_gain_mlp), ('blk', 'tok'))  65.8 us
    dot_general x6, matrix products, matmul(): return jnp.dot(left, right, preferred_element_type=jnp.float32)  59.1 us
    dot_general x6, matrix products, matmul_back(): lax.dot_general(left, right, (((1,), (1,)), ((), ())), preferred_element_...  52.1 us
    dot_general x6, matrix products, matmul_rows(): lax.dot_general(left, right, (((0,), (0,)), ((), ())), preferred_element_...  45.7 us
  transfers between devices with their start and end apart: 18, of which 13 were waited for; matrix products, arithmetic and copies ran while one was open for 37% of the time, Pallas kernels for 0%

commit v1 on v0

v1 whole, which is shorter than its diff:
```python
import functools
import math

import jax
import jax.numpy as jnp
from jax import lax
from jax.experimental import pallas as pl
from jax.experimental.pallas import tpu as pltpu
from jax.sharding import Mesh
from jax.sharding import PartitionSpec as P

EPSILON = 1e-06
MESH = pl.DeviceIdType.MESH
AXES = ("z", "y", "x", "core")
GELU_A = math.sqrt(2.0 / math.pi)
GELU_B = 0.044715
F32 = jnp.float32
BF16 = jnp.bfloat16


def dot_nn(left, right):
    return lax.dot_general(left, right, (((1,), (0,)), ((), ())), preferred_element_type=F32)


def dot_nt(left, right):
    return lax.dot_general(left, right, (((1,), (1,)), ((), ())), preferred_element_type=F32)


def dot_tn(left, right):
    return lax.dot_general(left, right, (((0,), (0,)), ((), ())), preferred_element_type=F32)


def gelu_parts(v):
    t = jnp.tanh(GELU_A * (v + GELU_B * v * v * v))
    return 0.5 * v * (1.0 + t), t


def gelu_slope(v, t):
    return 0.5 * (1.0 + t) + 0.5 * v * (1.0 - t * t) * (GELU_A * (1.0 + 3.0 * GELU_B * v * v))


def one_minus_exp(v):
    series = 1.0 + v * (1.0 / 9.0)
    for order in (8.0, 7.0, 6.0, 5.0, 4.0, 3.0, 2.0):
        series = 1.0 + v * (1.0 / order) * series
    return jnp.where(v > -0.5, -v * series, 1.0 - jnp.exp(v))


def around(axis, size, step):
    return {axis: lax.rem(lax.axis_index(axis) + (step + size), size)}


ROWS = 32
LANES = 128


def put(ref, here, value):
    for c in range(ref.shape[0]):
        ref[c, here, :] = value[:, c * LANES : (c + 1) * LANES]


def take(ref, here):
    return jnp.concatenate([ref[c, here, :] for c in range(ref.shape[0])], axis=1)


def forward_kernel(
    z_size,
    branch_in,
    gelu_in,
    masks,
    gate_a,
    gate_x,
    params,
    branch_out,
    conv_out,
    rate_out,
    admit_out,
    states_out,
    gated_out,
    enter_out,
    low,
    decay,
    local,
    product,
    totals,
    halo_sems,
    total_send,
    total_recv,
):
    rows, channels = branch_in.shape
    seg = rows // 8
    z = lax.axis_index("z")
    barrier = pltpu.get_barrier_semaphore()
    for step in range(1, z_size):
        pl.semaphore_signal(barrier, inc=1, device_id=around("z", z_size, step), device_id_type=MESH)
    pl.semaphore_wait(barrier, z_size - 1)
    halo = pltpu.make_async_remote_copy(
        src_ref=branch_in.at[pl.ds(rows - 8, 8)],
        dst_ref=branch_out.at[pl.ds(0, 8)],
        send_sem=halo_sems.at[0],
        recv_sem=halo_sems.at[1],
        device_id=around("z", z_size, 1),
        device_id_type=MESH,
    )
    halo.start()

    def move(i, carry):
        at = pl.multiple_of(i * ROWS, ROWS)
        branch_out[pl.ds(at + 8, ROWS), :] = branch_in[pl.ds(at, ROWS), :]
        return carry

    lax.fori_loop(0, rows // ROWS, move, 0)
    halo.wait()

    def conv(i, carry):
        at = pl.multiple_of(i * ROWS, ROWS)
        window = branch_out[pl.ds(at, ROWS + 8), :]
        mask = masks[pl.ds(at, ROWS), :]
        total = params[4:5, :] + params[0:1, :] * window[8:, :]
        for k in range(1, 4):
            total = total + params[k : k + 1, :] * window[8 - k : 8 - k + ROWS, :] * mask[:, k : k + 1]
        conv_out[pl.ds(at, ROWS), :] = total
        low[pl.ds(at, ROWS), :] = total.astype(BF16)
        return carry

    lax.fori_loop(0, rows // ROWS, conv, 0)

    def gates(i, carry):
        at = pl.multiple_of(i * 128, 128)
        rate_out[pl.ds(at, 128), :] = dot_nn(low[pl.ds(at, 128), :], gate_a[...])
        admit_out[pl.ds(at, 128), :] = dot_nn(low[pl.ds(at, 128), :], gate_x[...])
        return carry

    lax.fori_loop(0, rows // 128, gates, 0)

    def point(i, carry):
        at = pl.multiple_of(i * ROWS, ROWS)
        here = pl.ds(at, ROWS)
        restart = masks[here, 0:1] > 0.5
        rate = jax.nn.sigmoid(rate_out[here, :] + params[5:6, :])
        admit = jax.nn.sigmoid(admit_out[here, :] + params[6:7, :])
        log_decay = -8.0 * rate * params[8:9, :]
        scaling = jnp.where(restart, 1.0, jnp.sqrt(one_minus_exp(2.0 * log_decay)))
        rate_out[here, :] = rate
        admit_out[here, :] = admit
        put(decay, here, jnp.where(restart, 0.0, jnp.exp(log_decay)))
        put(local, here, scaling * admit * conv_out[here, :])
        return carry

    lax.fori_loop(0, rows // ROWS, point, 0)

    def scan(j, carry):
        state, prod = carry
        here = pl.ds(j, 8, stride=seg)
        rate = take(decay, here)
        state = rate * state + take(local, here)
        prod = prod * rate
        put(local, here, state)
        put(product, here, prod)
        return state, prod

    state, prod = lax.fori_loop(
        0, seg, scan, (jnp.zeros((8, channels), F32), jnp.ones((8, channels), F32))
    )

    def segments(entering):
        found = [entering]
        for s in range(8):
            found.append(prod[s : s + 1, :] * found[-1] + state[s : s + 1, :])
        return found

    whole = prod[0:1, :]
    for s in range(1, 8):
        whole = whole * prod[s : s + 1, :]
    totals[0, 0:1, :] = whole
    totals[0, 1:2, :] = segments(jnp.zeros((1, channels), F32))[-1]
    copies = []
    for step in range(1, z_size):
        copy = pltpu.make_async_remote_copy(
            src_ref=totals.at[0],
            dst_ref=totals.at[step],
            send_sem=total_send.at[step],
            recv_sem=total_recv.at[step],
            device_id=around("z", z_size, step),
            device_id_type=MESH,
        )
        copy.start()
        copies.append(copy)
    for copy in copies:
        copy.wait()
    entering = jnp.zeros((1, channels), F32)
    for step in range(z_size - 1, 0, -1):
        later = totals[step, 0:1, :] * entering + totals[step, 1:2, :]
        entering = jnp.where(z - step >= 0, later, entering)
    enter_out[...] = jnp.broadcast_to(entering, (8, channels))
    found = segments(entering)
    for s in range(8):
        base = s * seg

        def fix(i, carry):
            at = pl.multiple_of(base + i * ROWS, ROWS)
            here = pl.ds(at, ROWS)
            states = take(local, here) + take(product, here) * found[s]
            states_out[here, :] = states
            gated_out[here, :] = (states * gelu_parts(gelu_in[here, :])[0]).astype(BF16)
            return carry

        lax.fori_loop(0, seg // ROWS, fix, 0)


def backward_kernel(
    z_size,
    g_gated,
    gelu_in,
    branch_in,
    conv_in,
    rate_in,
    admit_in,
    states_in,
    enter_in,
    masks,
    gate_a,
    gate_x,
    params,
    g_gelu_out,
    g_branch_out,
    rate_low,
    admit_low,
    conv_low,
    small_out,
    decay,
    local,
    product,
    conv_grad,
    totals,
    halo_sems,
    total_send,
    total_recv,
):
    rows, channels = g_gated.shape
    seg = rows // 8
    z = lax.axis_index("z")
    barrier = pltpu.get_barrier_semaphore()
    for step in range(1, z_size):
        pl.semaphore_signal(barrier, inc=1, device_id=around("z", z_size, step), device_id_type=MESH)
    pl.semaphore_wait(barrier, z_size - 1)

    def point(i, carry):
        at = pl.multiple_of(i * ROWS, ROWS)
        here = pl.ds(at, ROWS)
        restart = masks[here, 0:1] > 0.5
        grads = g_gated[here, :]
        value, tang = gelu_parts(gelu_in[here, :])
        g_gelu_out[here, :] = (grads * states_in[here, :] * gelu_slope(gelu_in[here, :], tang)).astype(BF16)
        put(local, here, grads * value)
        put(decay, here, jnp.where(restart, 0.0, jnp.exp(-8.0 * rate_in[here, :] * params[8:9, :])))
        return carry

    lax.fori_loop(0, rows // ROWS, point, 0)

    def scan(i, carry):
        j = seg - 1 - i
        coming, prod = carry
        here = pl.ds(j, 8, stride=seg)
        rate = take(decay, here)
        total = take(local, here) + coming
        put(local, here, total)
        put(product, here, prod)
        return rate * total, prod * rate

    coming, prod = lax.fori_loop(
        0, seg, scan, (jnp.zeros((8, channels), F32), jnp.ones((8, channels), F32))
    )

    def segments(entering):
        found = [None] * 8 + [entering]
        for s in range(7, -1, -1):
            found[s] = prod[s : s + 1, :] * found[s + 1] + coming[s : s + 1, :]
        return found

    whole = prod[0:1, :]
    for s in range(1, 8):
        whole = whole * prod[s : s + 1, :]
    totals[0, 0:1, :] = whole
    totals[0, 1:2, :] = segments(jnp.zeros((1, channels), F32))[0]
    copies = []
    for step in range(1, z_size):
        copy = pltpu.make_async_remote_copy(
            src_ref=totals.at[0],
            dst_ref=totals.at[step],
            send_sem=total_send.at[step],
            recv_sem=total_recv.at[step],
            device_id=around("z", z_size, -step),
            device_id_type=MESH,
        )
        copy.start()
        copies.append(copy)
    for copy in copies:
        copy.wait()
    entering = jnp.zeros((1, channels), F32)
    for step in range(z_size - 1, 0, -1):
        later = totals[step, 0:1, :] * entering + totals[step, 1:2, :]
        entering = jnp.where(z + step < z_size, later, entering)
    found = segments(entering)
    sums = (jnp.zeros((1, channels), F32),) * 3
    for s in range(8):
        base = s * seg
        before_first = enter_in[0:1, :] if s == 0 else states_in[base - 1 : base, :]

        def fix(i, carry):
            rate_sum, admit_sum, decay_sum, before_block = carry
            at = pl.multiple_of(base + i * ROWS, ROWS)
            here = pl.ds(at, ROWS)
            running = masks[here, 0:1] < 0.5
            states = states_in[here, :]
            before = jnp.concatenate([before_block, states[: ROWS - 1, :]], axis=0)
            carried = take(local, here) + take(product, here) * found[s + 1]
            rate = rate_in[here, :]
            admit = admit_in[here, :]
            conv = conv_in[here, :]
            spread = take(decay, here)
            scaling = jnp.where(running, jnp.sqrt(one_minus_exp(-16.0 * rate * params[8:9, :])), 1.0)
            driven = admit * conv
            g_log = jnp.where(
                running, carried * (before * spread - driven * spread * spread / scaling), 0.0
            )
            g_rate = g_log * (-8.0 * params[8:9, :]) * rate * (1.0 - rate)
            scaled = carried * scaling * admit
            g_admit = scaled * conv * (1.0 - admit)
            rate_low[here, :] = g_rate.astype(BF16)
            admit_low[here, :] = g_admit.astype(BF16)
            conv_low[here, :] = conv.astype(BF16)
            conv_grad[here, :] = scaled
            return (
                rate_sum + jnp.sum(g_rate, axis=0, keepdims=True),
                admit_sum + jnp.sum(g_admit, axis=0, keepdims=True),
                decay_sum + jnp.sum(g_log * rate, axis=0, keepdims=True),
                states[ROWS - 1 :, :],
            )

        result = lax.fori_loop(0, seg // ROWS, fix, sums + (before_first,))
        sums = result[:3]

    def gates(i, carry):
        at = pl.multiple_of(i * 128, 128)
        here = pl.ds(at, 128)
        conv_grad[here, :] = (
            conv_grad[here, :]
            + dot_nt(rate_low[here, :], gate_a[...])
            + dot_nt(admit_low[here, :], gate_x[...])
        )
        return carry

    lax.fori_loop(0, rows // 128, gates, 0)
    halo = pltpu.make_async_remote_copy(
        src_ref=conv_grad.at[pl.ds(0, 8)],
        dst_ref=conv_grad.at[pl.ds(rows, 8)],
        send_sem=halo_sems.at[0],
        recv_sem=halo_sems.at[1],
        device_id=around("z", z_size, -1),
        device_id_type=MESH,
    )
    halo.start()
    halo.wait()

    def conv(i, carry):
        at = pl.multiple_of(i * ROWS, ROWS)
        grads = conv_grad[pl.ds(at, ROWS + 8), :]
        mask = masks[pl.ds(at, ROWS + 8), :]
        window = branch_in[pl.ds(at, ROWS + 8), :]
        own = grads[:ROWS, :]
        total = params[0:1, :] * own
        new = [carry[0] + jnp.sum(own * window[8:, :], axis=0, keepdims=True)]
        for k in range(1, 4):
            held = grads * mask[:, k : k + 1]
            total = total + params[k : k + 1, :] * held[k : k + ROWS, :]
            new.append(
                carry[k] + jnp.sum(held[:ROWS, :] * window[8 - k : 8 - k + ROWS, :], axis=0, keepdims=True)
            )
        new.append(carry[4] + jnp.sum(own, axis=0, keepdims=True))
        g_branch_out[pl.ds(at, ROWS), :] = total.astype(BF16)
        return tuple(new)

    taps = lax.fori_loop(0, rows // ROWS, conv, (jnp.zeros((1, channels), F32),) * 5)
    for k in range(5):
        small_out[k : k + 1, :] = taps[k]
    small_out[5:6, :] = sums[0]
    small_out[6:7, :] = sums[1]
    small_out[7:8, :] = sums[2] * 8.0 * params[9:10, :]


def placed(step):
    return ((step % 4) * 2 + step // 4) * 256


class Links:
    def __init__(self, send, recv):
        self.send, self.recv, self.used = send, recv, 0

    def start(self, src, dst, axis, step):
        size = lax.axis_size(axis)
        copy = pltpu.make_async_remote_copy(
            src_ref=src,
            dst_ref=dst,
            send_sem=self.send.at[self.used],
            recv_sem=self.recv.at[self.used],
            device_id=around(axis, size, step),
            device_id_type=MESH,
        )
        self.used += 1
        copy.start()
        return copy

    def local(self, src, dst):
        copy = pltpu.make_async_copy(src, dst, self.send.at[self.used])
        self.used += 1
        copy.start()
        return copy


def greet(reach):
    barrier = pltpu.get_barrier_semaphore()
    total = 0
    for axis, steps in reach:
        for step in steps:
            pl.semaphore_signal(
                barrier, inc=1, device_id=around(axis, lax.axis_size(axis), step), device_id_type=MESH
            )
            total += 1
    pl.semaphore_wait(barrier, total)


EVERYONE = (("y", (1, 2, 3)), ("x", (1, 2, 3)), ("z", (1, 2, 3)), ("core", (1,)))


def run(*tasks):
    waiting = list(tasks)
    while waiting:
        for task in list(waiting):
            try:
                next(task)
            except StopIteration:
                waiting.remove(task)


def gather_weight(links, own, full):
    z, x, core = lax.axis_index("z"), lax.axis_index("x"), lax.axis_index("core")
    rows = own.shape[0]
    half = rows // 2
    mine = pl.ds(pl.multiple_of((core * 4 + x) * 256, 256), 256)
    ours = pl.ds(pl.multiple_of(core * 1024, 1024), 1024)
    top, low = pl.ds(0, half), pl.ds(half, rows - half)
    sent = []
    here = links.local(own, full.at[z, :, mine])
    first_a = [links.start(own.at[top], full.at[z, top, mine], "x", s) for s in (1, 3, 2)]
    first_b = [links.start(own.at[low], full.at[z, low, mine], "z", s) for s in (1, 3, 2)]
    sent += first_a + first_b
    yield
    here.wait()
    for copy in first_a:
        copy.wait_recv()
    block = full.at[z, top, ours]
    second_a = [links.start(block, block, "z", s) for s in (1, -1)]
    for copy in first_b:
        copy.wait_recv()
    block = full.at[:, low, mine]
    second_b = [links.start(block, block, "x", s) for s in (1, -1)]
    sent += second_a + second_b
    yield
    relays = []
    for way in (0, 1):
        step = 1 if way == 0 else -1
        origin = lax.rem(z - step + 4, 4)
        second_a[way].wait_recv()
        half_lanes = pl.ds(pl.multiple_of(core * 1024 + way * 512, 512), 512)
        block = full.at[origin, top, half_lanes]
        relays.append(links.start(block, block, "z", step))
        origin = lax.rem(x - step + 4, 4)
        second_b[way].wait_recv()
        lanes = pl.ds(pl.multiple_of((core * 4 + origin) * 256, 256), 256)
        block = full.at[pl.ds(2 * way, 2), low, lanes]
        relays.append(links.start(block, block, "x", step))
    sent += relays
    yield
    for copy in relays:
        copy.wait_recv()
    block = full.at[:, :, ours]
    last = links.start(block, block, "core", 1)
    sent.append(last)
    yield
    last.wait_recv()
    for copy in sent:
        copy.wait_send()


GATHER_SEMS = 16


def gather_rows(links, seq):
    y = lax.axis_index("y")
    own = seq.at[y]
    first = [links.start(own, own, "y", s) for s in (1, -1)]
    yield
    relays = []
    for way in (0, 1):
        step = 1 if way == 0 else -1
        first[way].wait_recv()
        block = seq.at[lax.rem(y - step + 4, 4), :, pl.ds(way * 1024, 1024)]
        relays.append(links.start(block, block, "y", step))
    yield
    for copy in relays:
        copy.wait_recv()
    for copy in first + relays:
        copy.wait_send()


def add_rows(out, terms, dtype=None):
    count = out.shape[0] // 16

    def body(i, carry):
        here = pl.ds(pl.multiple_of(i * 16, 16), 16)
        total = terms[0][here, :].astype(F32)
        for term in terms[1:]:
            total = total + term[here, :].astype(F32)
        out[here, :] = total.astype(out.dtype)
        return carry

    lax.fori_loop(0, count, body, 0)


def scatter_rows(links, part, far, near, out):
    y = lax.axis_index("y")
    across = part.at[lax.rem(y + 2, 4)]
    first = [
        links.start(across.at[:, pl.ds(way * 1024, 1024)], far.at[way], "y", 1 - 2 * way) for way in (0, 1)
    ]
    yield
    second = []
    for way in (0, 1):
        step = 1 - 2 * way
        first[way].wait_recv()
        chunk = part.at[lax.rem(y + step + 4, 4)]
        lanes = pl.ds(way * 1024, 1024)
        add_rows(chunk.at[:, lanes], [chunk.at[:, lanes], far.at[way]])
        second.append(links.start(chunk, near.at[way], "y", step))
    yield
    for copy in second:
        copy.wait_recv()
    add_rows(out, [part.at[y], near.at[0], near.at[1]])
    for copy in first + second:
        copy.wait_send()


def scatter_weight(links, part, own, mate, heavy_a, heavy_b, light_a, light_b, out):
    z, x, core = lax.axis_index("z"), lax.axis_index("x"), lax.axis_index("core")
    rows = part.shape[1]
    half = rows // 2
    top, low = pl.ds(0, half), pl.ds(half, rows - half)
    theirs = pl.ds(pl.multiple_of((1 - core) * 1024, 1024), 1024)
    ours = pl.ds(pl.multiple_of(core * 1024, 1024), 1024)
    here = links.local(part.at[:, :, ours], own)
    across = links.start(part.at[:, :, theirs], mate, "core", 1)
    yield
    here.wait()
    across.wait_recv()
    for block in range(4):
        add_rows(own.at[block], [own.at[block], mate.at[block]])
    first_a, first_b = [], []
    for i, step in enumerate((1, 3, 2)):
        to_z = lax.rem(z + step, 4)
        first_a.append(links.start(own.at[to_z, top, :], heavy_a.at[i], "z", step))
        to_x = pl.ds(pl.multiple_of(lax.rem(x + step, 4) * 256, 256), 256)
        first_b.append(links.start(own.at[:, low, to_x], heavy_b.at[i], "x", step))
    yield
    for copy in first_a:
        copy.wait_recv()
    mine_a = own.at[z, top, :]
    add_rows(mine_a, [mine_a] + [heavy_a.at[i] for i in range(3)])
    second = []
    for i, step in enumerate((1, 3, 2)):
        to_x = pl.ds(pl.multiple_of(lax.rem(x + step, 4) * 256, 256), 256)
        second.append(links.start(own.at[z, top, to_x], light_a.at[i], "x", step))
    for copy in first_b:
        copy.wait_recv()
    my_x = pl.ds(pl.multiple_of(x * 256, 256), 256)
    for block in range(4):
        mine_b = own.at[block, low, my_x]
        add_rows(mine_b, [mine_b] + [heavy_b.at[i, block] for i in range(3)])
    for i, step in enumerate((1, 3, 2)):
        to_z = lax.rem(z + step, 4)
        second.append(links.start(own.at[to_z, low, my_x], light_b.at[i], "z", step))
    yield
    for copy in second:
        copy.wait_recv()
    add_rows(out.at[top], [own.at[z, top, my_x]] + [light_a.at[i] for i in range(3)])
    add_rows(out.at[low], [own.at[z, low, my_x]] + [light_b.at[i] for i in range(3)])
    for copy in [across] + first_a + first_b + second:
        copy.wait_send()


SCATTER_SEMS = 16


def scatter_scratch(rows):
    half = rows // 2
    return [
        pltpu.VMEM((4, rows, 1024), BF16),
        pltpu.VMEM((4, rows, 1024), BF16),
        pltpu.VMEM((3, half, 1024), BF16),
        pltpu.VMEM((3, 4, half, 256), BF16),
        pltpu.VMEM((3, half, 256), BF16),
        pltpu.VMEM((3, half, 256), BF16),
    ]


def sum_everywhere(links, slots, axis):
    size = lax.axis_size(axis)
    own = slots.at[lax.axis_index(axis)]
    copies = [links.start(own, own, axis, s) for s in range(1, size)]
    yield
    for copy in copies:
        copy.wait_recv()
    for copy in copies:
        copy.wait_send()


STRIP = 16


def placed_rows(ref, here):
    return jnp.concatenate([ref[here, pl.ds(placed(p), 256)] for p in range(8)], axis=1)


def restore_rows(ref, here, value):
    for p in range(8):
        ref[here, pl.ds(placed(p), 256)] = value[:, p * 256 : (p + 1) * 256]


def strips(count, body, carry=0):
    def step(i, carry):
        return body(pl.ds(pl.multiple_of(i * STRIP, STRIP), STRIP), carry)

    return lax.fori_loop(0, count // STRIP, step, carry)


def inverse_rms(values):
    return lax.rsqrt(jnp.mean(values * values, axis=-1, keepdims=True) + EPSILON)


def norm_back(grads, values, scale, gain):
    held = grads * gain
    return scale * held - values * (scale * scale * scale) * jnp.mean(held * values, axis=-1, keepdims=True)


def first_kernel(widths, x_in, gain, weights, seq, branch, gelu, out, normed, send, recv):
    links = Links(send, recv)
    y = lax.axis_index("y")
    greet(EVERYONE)
    tasks, at = [], 0
    for full, width in zip((branch, gelu, out), widths):
        tasks.append(gather_weight(links, weights.at[pl.ds(at, width)], full))
        at += width

    def rows():
        gains = placed_rows(gain, slice(None))

        def body(here, carry):
            values = placed_rows(x_in, here).astype(F32)
            normed[here, :] = (values * inverse_rms(values) * gains).astype(BF16)
            return carry

        strips(x_in.shape[0], body)
        copy = links.local(normed, seq.at[y])
        copy.wait()
        yield from gather_rows(links, seq)

    run(*tasks, rows())


def middle_kernel(
    widths, skip, part, x_in, cot, gain, weights, mixed, seq_mlp, seq_grad, gate, up, down,
    far, near, normed, cot_placed, send, recv,
):
    links = Links(send, recv)
    y = lax.axis_index("y")
    count = x_in.shape[0]
    greet(EVERYONE)
    tasks, at = [], skip
    for full, width in zip((gate, up, down), widths):
        tasks.append(gather_weight(links, weights.at[pl.ds(at, width)], full))
        at += width

    def rows():
        yield from scatter_rows(links, part, far, near, mixed)
        gains = placed_rows(gain, slice(None))

        def body(here, carry):
            values = placed_rows(x_in, here).astype(F32) + mixed[here, :]
            mixed[here, :] = values
            normed[here, :] = (values * inverse_rms(values) * gains).astype(BF16)
            cot_placed[here, :] = placed_rows(cot, here)
            return carry

        strips(count, body)
        own_mlp = links.local(normed, seq_mlp.at[y])
        own_grad = links.local(cot_placed, seq_grad.at[y])
        own_mlp.wait()
        yield from gather_rows(links, seq_mlp)
        own_grad.wait()
        yield from gather_rows(links, seq_grad)

    run(rows(), *tasks)


def third_kernel(
    part_out, part_back, grad_gate, grad_up, grad_down, mixed, cot, gain,
    output, g_mixed, seq_mixed, gate_out, up_out, down_out, gain_out,
    far, near, total, low, far_out, near_out, *rest,
):
    send, recv = rest[-2:]
    links = Links(send, recv)
    y = lax.axis_index("y")
    count, model = mixed.shape
    greet(EVERYONE)
    tasks = []
    for i, (part, out) in enumerate(
        ((grad_down, down_out), (grad_gate, gate_out), (grad_up, up_out))
    ):
        tasks.append(scatter_weight(links, part, *rest[6 * i : 6 * i + 6], out))

    def rows():
        yield from scatter_rows(links, part_back, far, near, total)
        gains = placed_rows(gain, slice(None))

        def body(here, carry):
            values = mixed[here, :]
            back = total[here, :]
            scale = inverse_rms(values)
            grads = placed_rows(cot, here).astype(F32) + norm_back(back, values, scale, gains)
            g_mixed[here, :] = grads
            low[here, :] = grads.astype(BF16)
            return carry + jnp.sum(back * values * scale, axis=0, keepdims=True)

        sums = strips(count, body, jnp.zeros((1, model), F32))
        restore_rows(gain_out, slice(None), jnp.broadcast_to(sums, (8, model)))
        copy = links.local(low, seq_mixed.at[y])
        copy.wait()
        yield from gather_rows(links, seq_mixed)
        yield from scatter_rows(links, part_out, far_out, near_out, total)

        def last(here, carry):
            restore_rows(output, here, (mixed[here, :] + total[here, :]).astype(BF16))
            return carry

        strips(count, last)

    run(rows(), *tasks)


def fourth_kernel(
    part, grad_branch, grad_gelu, grad_out, g_mixed, x_in, gain, gain_mlp, small,
    g_inputs, branch_out, gelu_out, out_out, small_out, gain_out,
    far, near, total, small_z, small_x, small_core, gain_slots, *rest,
):
    send, recv = rest[-2:]
    links = Links(send, recv)
    count, model = g_mixed.shape
    greet(EVERYONE)
    tasks = []
    for i, (weight, out) in enumerate(
        ((grad_branch, branch_out), (grad_gelu, gelu_out), (grad_out, out_out))
    ):
        tasks.append(scatter_weight(links, weight, *rest[6 * i : 6 * i + 6], out))
    z, x, core = lax.axis_index("z"), lax.axis_index("x"), lax.axis_index("core")

    def smalls():
        copies = []
        for i, step in enumerate((1, 3, 2)):
            copies.append(links.start(small.at[lax.rem(z + step, 4)], small_z.at[i], "z", step))
        yield
        for copy in copies:
            copy.wait_recv()
        add_rows(small_x.at[x], [small.at[z]] + [small_z.at[i] for i in range(3)])
        yield from sum_everywhere(links, small_x, "x")
        add_rows(small_core.at[core], [small_x.at[i] for i in range(4)])
        yield from sum_everywhere(links, small_core, "core")
        add_rows(small_out, [small_core.at[0], small_core.at[1]])
        for copy in copies:
            copy.wait_send()

    def rows():
        yield from scatter_rows(links, part, far, near, total)
        gains = placed_rows(gain, slice(None))

        def body(here, carry):
            values = placed_rows(x_in, here).astype(F32)
            back = total[here, :]
            scale = inverse_rms(values)
            grads = g_mixed[here, :] + norm_back(back, values, scale, gains)
            restore_rows(g_inputs, here, grads)
            return carry + jnp.sum(back * values * scale, axis=0, keepdims=True)

        sums = strips(count, body, jnp.zeros((1, model), F32))
        restore_rows(gain_out, slice(0, 1), sums)
        gain_out[1:2, :] = gain_mlp[0:1, :]
        gain_out[2:8, :] = jnp.zeros((6, model), F32)
        for n, axis in enumerate(("y", "z", "x", "core")):
            size = lax.axis_size(axis)
            slots = gain_slots.at[n]
            slots[lax.axis_index(axis)] = gain_out[...]
            yield from sum_everywhere(links, slots.at[pl.ds(0, size)], axis)
            total_now = slots[0]
            for i in range(1, size):
                total_now = total_now + slots[i]
            gain_out[...] = total_now

    run(rows(), smalls(), *tasks)


def any_space(count):
    return [pl.BlockSpec(memory_space=pl.ANY)] * count


def vmem(count):
    return [pl.BlockSpec(memory_space=pltpu.VMEM)] * count


def shape(dims, dtype):
    return jax.ShapeDtypeStruct(dims, dtype)


def sems(count):
    return [pltpu.SemaphoreType.DMA((count,)), pltpu.SemaphoreType.DMA((count,))]


def options(number, mib=56):
    return pltpu.CompilerParams(
        collective_id=number, has_side_effects=True, vmem_limit_bytes=mib * 2**20
    )


def call_first(x_in, gain, weights, widths):
    count, model = x_in.shape
    return pl.pallas_call(
        functools.partial(first_kernel, widths),
        out_shape=[shape((4, count, model), BF16)] + [shape((4, w, model), BF16) for w in widths],
        in_specs=vmem(2) + any_space(1),
        out_specs=any_space(4),
        scratch_shapes=[pltpu.VMEM((count, model), BF16)] + sems(3 * GATHER_SEMS + 8),
        compiler_params=options(3),
    )(x_in, gain, weights)


def call_middle(part, x_in, cot, gain, weights, widths, skip):
    count, model = x_in.shape
    seq = shape((4, count, model), BF16)
    return pl.pallas_call(
        functools.partial(middle_kernel, widths, skip),
        out_shape=[shape((count, model), F32), seq, seq] + [shape((4, w, model), BF16) for w in widths],
        in_specs=vmem(4) + any_space(1),
        out_specs=vmem(1) + any_space(5),
        scratch_shapes=[
            pltpu.VMEM((2, count, model // 2), BF16),
            pltpu.VMEM((2, count, model), BF16),
            pltpu.VMEM((count, model), BF16),
            pltpu.VMEM((count, model), BF16),
        ]
        + sems(3 * GATHER_SEMS + 16),
        compiler_params=options(4),
    )(part, x_in, cot, gain, weights)


def call_third(part_out, part_back, grad_gate, grad_up, grad_down, mixed, cot, gain):
    count, model = mixed.shape
    width = grad_gate.shape[1]
    final = shape((width, 256), F32)
    return pl.pallas_call(
        third_kernel,
        out_shape=[
            shape((count, model), BF16),
            shape((count, model), F32),
            shape((4, count, model), BF16),
            final,
            final,
            final,
            shape((8, model), F32),
        ],
        in_specs=vmem(2) + any_space(3) + vmem(3),
        out_specs=vmem(2) + any_space(1) + vmem(4),
        scratch_shapes=[
            pltpu.VMEM((2, count, model // 2), BF16),
            pltpu.VMEM((2, count, model), BF16),
            pltpu.VMEM((count, model), F32),
            pltpu.VMEM((count, model), BF16),
            pltpu.VMEM((2, count, model // 2), BF16),
            pltpu.VMEM((2, count, model), BF16),
        ]
        + scatter_scratch(width) * 3
        + sems(3 * SCATTER_SEMS + 16),
        compiler_params=options(5),
    )(part_out, part_back, grad_gate, grad_up, grad_down, mixed, cot, gain)


def call_fourth(part, grad_branch, grad_gelu, grad_out, g_mixed, x_in, gain, gain_mlp, small):
    count, model = g_mixed.shape
    width = grad_out.shape[1]
    final = shape((width, 256), F32)
    packed = small.shape[1:]
    return pl.pallas_call(
        fourth_kernel,
        out_shape=[
            shape((count, model), F32),
            final,
            final,
            final,
            shape(packed, F32),
            shape((8, model), F32),
        ],
        in_specs=vmem(1) + any_space(3) + vmem(5),
        out_specs=vmem(6),
        scratch_shapes=[
            pltpu.VMEM((2, count, model // 2), BF16),
            pltpu.VMEM((2, count, model), BF16),
            pltpu.VMEM((count, model), F32),
            pltpu.VMEM((3,) + packed, BF16),
            pltpu.VMEM((4,) + packed, BF16),
            pltpu.VMEM((2,) + packed, BF16),
            pltpu.VMEM((4, 4, 8, model), F32),
        ]
        + scatter_scratch(width) * 3
        + sems(3 * SCATTER_SEMS + 32),
        compiler_params=options(6),
    )(part, grad_branch, grad_gelu, grad_out, g_mixed, x_in, gain, gain_mlp, small)


def recurrence_forward(branch, gelu_pre, masks, gate_a, gate_x, params):
    z_size = lax.axis_size("z")
    rows, channels = branch.shape
    wide = jax.ShapeDtypeStruct((rows, channels), F32)
    return pl.pallas_call(
        functools.partial(forward_kernel, z_size),
        out_shape=[
            jax.ShapeDtypeStruct((rows + 8, channels), F32),
            wide,
            wide,
            wide,
            wide,
            jax.ShapeDtypeStruct((rows, channels), BF16),
            jax.ShapeDtypeStruct((8, channels), F32),
        ],
        in_specs=vmem(6),
        out_specs=vmem(7),
        scratch_shapes=[
            pltpu.VMEM((rows, channels), BF16),
            pltpu.VMEM((channels // LANES, rows, LANES), F32),
            pltpu.VMEM((channels // LANES, rows, LANES), F32),
            pltpu.VMEM((channels // LANES, rows, LANES), F32),
            pltpu.VMEM((z_size, 8, channels), F32),
            pltpu.SemaphoreType.DMA((2,)),
            pltpu.SemaphoreType.DMA((z_size,)),
            pltpu.SemaphoreType.DMA((z_size,)),
        ],
        compiler_params=pltpu.CompilerParams(
            collective_id=1, has_side_effects=True, vmem_limit_bytes=48 * 2**20
        ),
    )(branch, gelu_pre, masks, gate_a, gate_x, params)


def recurrence_backward(g_gated, gelu_pre, branch, conv, rate, admit, states, enter, masks, gate_a, gate_x, params):
    z_size = lax.axis_size("z")
    rows, channels = g_gated.shape
    low = jax.ShapeDtypeStruct((rows, channels), BF16)
    return pl.pallas_call(
        functools.partial(backward_kernel, z_size),
        out_shape=[low, low, low, low, low, jax.ShapeDtypeStruct((8, channels), F32)],
        in_specs=vmem(12),
        out_specs=vmem(6),
        scratch_shapes=[
            pltpu.VMEM((channels // LANES, rows, LANES), F32),
            pltpu.VMEM((channels // LANES, rows, LANES), F32),
            pltpu.VMEM((channels // LANES, rows, LANES), F32),
            pltpu.VMEM((rows + 8, channels), F32),
            pltpu.VMEM((z_size, 8, channels), F32),
            pltpu.SemaphoreType.DMA((2,)),
            pltpu.SemaphoreType.DMA((z_size,)),
            pltpu.SemaphoreType.DMA((z_size,)),
        ],
        compiler_params=pltpu.CompilerParams(
            collective_id=2, has_side_effects=True, vmem_limit_bytes=48 * 2**20
        ),
    )(g_gated, gelu_pre, branch, conv, rate, admit, states, enter, masks, gate_a, gate_x, params)


def block_diagonal(blocks):
    count, size, _ = blocks.shape
    spread = blocks[:, :, None, :] * jnp.eye(count, dtype=blocks.dtype)[:, None, :, None]
    return spread.reshape(count * size, count * size)


def diagonal_blocks(square, count):
    size = square.shape[0] // count
    return jnp.stack([square[i * size : (i + 1) * size, i * size : (i + 1) * size] for i in range(count)])


def on_device(
    inputs,
    resets,
    gain_rec,
    w_branch,
    w_gelu,
    conv_weight,
    conv_bias,
    gate_a_weight,
    gate_a_bias,
    gate_x_weight,
    gate_x_bias,
    decay_param,
    w_out,
    gain_mlp,
    w_gate,
    w_up,
    w_down,
    cotangent,
):
    shard, _, model = inputs.shape
    z_size, y_size = lax.axis_size("z"), lax.axis_size("y")
    z = lax.axis_index("z")
    rows = shard * y_size
    length = resets.shape[0]
    flags = jnp.pad(resets.reshape(length).astype(F32), (8, 8), constant_values=1.0)
    window = lax.dynamic_slice(flags, (z * rows,), (rows + 16,))
    keep = 1.0 - window
    first = keep[8:]
    second = first * keep[7:-1]
    third = second * keep[6:-2]
    masks = jnp.stack([window[8:], first, second, third] + [jnp.zeros_like(first)] * 4, axis=1)

    vectors = jnp.concatenate(
        [conv_weight, jnp.stack([conv_bias, gate_a_bias, gate_x_bias, decay_param])], axis=0
    )
    vectors = lax.all_gather(vectors, "z", axis=0).transpose(1, 0, 2).reshape(8, -1)
    soft = jax.nn.softplus(-vectors[7:8])
    slope = jax.nn.sigmoid(-vectors[7:8])
    params = jnp.concatenate([vectors, soft, slope, jnp.zeros((6, vectors.shape[1]), F32)], axis=0)
    gates = lax.all_gather(jnp.concatenate([gate_a_weight, gate_x_weight]), "z", axis=0)
    gate_a = block_diagonal(gates[:, 0])
    gate_x = block_diagonal(gates[:, 1])

    rec, mlp = w_branch.shape[1], w_gate.shape[1]
    weights = jnp.concatenate([w_branch, w_gelu, w_out, w_gate, w_up, w_down], axis=1).T
    gain_rec = gain_rec.reshape(1, model)
    gain_mlp = gain_mlp.reshape(1, model)

    def whole(parts):
        return parts.reshape(-1, parts.shape[-1])

    def split(full):
        return full.astype(BF16).reshape(y_size, -1, model)

    flat = inputs.reshape(shard, model)
    cot = cotangent.reshape(shard, model)
    seq_normed, full_branch, full_gelu, full_out = map(
        whole, call_first(flat, gain_rec, weights, (rec,) * 3)
    )
    branch = dot_nt(seq_normed, full_branch)
    gelu_pre = dot_nt(seq_normed, full_gelu)
    branch_held, conv, rate, admit, states, gated, enter = recurrence_forward(
        branch, gelu_pre, masks, gate_a, gate_x, params
    )
    mixed, seq_mlp, seq_grad, full_gate, full_up, full_down = map(
        whole,
        call_middle(
            split(dot_nn(gated, full_out)), flat, cot, gain_mlp, weights, (mlp,) * 3, 3 * rec
        ),
    )
    gate_pre = dot_nt(seq_mlp, full_gate)
    up_pre = dot_nt(seq_mlp, full_up)
    gate_value, gate_tang = gelu_parts(gate_pre)
    hidden = (gate_value * up_pre).astype(BF16)
    g_hidden = dot_nt(seq_grad, full_down)
    g_gate = (g_hidden * up_pre * gelu_slope(gate_pre, gate_tang)).astype(BF16)
    g_up = (g_hidden * gate_value).astype(BF16)
    part_out = split(dot_nn(hidden, full_down))
    part_back = split(dot_nn(g_gate, full_gate) + dot_nn(g_up, full_up))
    output, g_mixed, seq_mixed, grad_gate, grad_up, grad_down, gain_part = call_third(
        part_out,
        part_back,
        split(dot_tn(g_gate, seq_mlp)),
        split(dot_tn(g_up, seq_mlp)),
        split(dot_tn(hidden, seq_grad)),
        mixed,
        cot,
        gain_mlp,
    )
    seq_mixed = whole(seq_mixed)
    g_gated = dot_nt(seq_mixed, full_out)
    g_gelu, g_branch, rate_low, admit_low, conv_low, small = recurrence_backward(
        g_gated, gelu_pre, branch_held, conv, rate, admit, states, enter, masks, gate_a, gate_x, params
    )
    blocks_a = diagonal_blocks(dot_tn(conv_low, rate_low), z_size).reshape(z_size, -1)
    blocks_x = diagonal_blocks(dot_tn(conv_low, admit_low), z_size).reshape(z_size, -1)
    vectors_back = small.reshape(8, z_size, rec).transpose(1, 0, 2).reshape(z_size, -1)
    packed = jnp.concatenate([blocks_a, blocks_x, vectors_back], axis=1).astype(BF16)
    packed = jnp.pad(packed, ((0, 0), (0, -packed.shape[1] % 4096))).reshape(z_size, -1, 256)
    g_inputs, grad_branch, grad_gelu, grad_out, packed, gains = call_fourth(
        split(dot_nn(g_branch, full_branch) + dot_nn(g_gelu, full_gelu)),
        split(dot_tn(g_branch, seq_normed)),
        split(dot_tn(g_gelu, seq_normed)),
        split(dot_tn(gated, seq_mixed)),
        g_mixed,
        flat,
        gain_rec,
        gain_part,
        packed,
    )
    packed = packed.reshape(-1)
    block = rec * rec
    vector = packed[2 * block : 2 * block + 8 * rec].reshape(8, rec)
    return (
        output.reshape(shard, 1, model),
        g_inputs.reshape(shard, 1, model),
        gains[0],
        grad_branch.T,
        grad_gelu.T,
        vector[:4],
        vector[4],
        packed[:block].reshape(1, rec, rec),
        vector[5],
        packed[block : 2 * block].reshape(1, rec, rec),
        vector[6],
        vector[7],
        grad_out.T,
        gains[1],
        grad_gate.T,
        grad_up.T,
        grad_down.T,
    )


def solution(mesh):
    sizes = {"blk": mesh.shape["blk"], "tok": mesh.shape["tok"]}
    side = math.isqrt(sizes["blk"])
    grid = Mesh(mesh.devices.reshape(side, side, sizes["tok"] // 2, 2), AXES)
    blk, tok = ("z", "y"), ("x", "core")
    in_specs = (
        P(blk, tok, None),
        P(None, tok),
        P(),
        P(tok, blk),
        P(tok, blk),
        P(None, blk),
        P(blk),
        P(blk, None, None),
        P(blk),
        P(blk, None, None),
        P(blk),
        P(blk),
        P(tok, blk),
        P(),
        P(tok, blk),
        P(tok, blk),
        P(tok, blk),
        P(blk, tok, None),
    )
    out_specs = (
        P(blk, tok, None),
        P(blk, tok, None),
        P(),
        P(tok, blk),
        P(tok, blk),
        P(None, blk),
        P(blk),
        P(blk, None, None),
        P(blk),
        P(blk, None, None),
        P(blk),
        P(blk),
        P(tok, blk),
        P(),
        P(tok, blk),
        P(tok, blk),
        P(tok, blk),
    )
    return jax.shard_map(
        on_device, mesh=grid, in_specs=in_specs, out_specs=out_specs, check_vma=False
    )
```

time: 1610 us -> 481 us (0.30)
  waiting for transfers between devices: 671 us -> 0 us
  local copies, waits for them, and re-layouts: 461 us -> 27 us
  Pallas kernels: 0 us -> 330 us
  other arithmetic: 165 us -> 5.39 us
  blocking collectives: 109 us -> 21.7 us
  matrix products: 165 us -> 87.5 us
  between operations: 18.3 us -> 1.4 us
    reduce_scatter x10 -> x0, waiting for transfers between devices: 424 us -> none  [the longest x4 342 us: scattered(): lax.psum_scatter(whole, axis, scatter_dimension=0, tiled=True)]
    pad x50 -> x0, local copies, waits for them, and re-layouts: 338 us -> none  [linear_scan(): inclusive = lax.associative_scan(combine, (product, running), axis=0)[1]]
    pallas_call x0 -> x6, Pallas kernels: none -> 330 us  [the longest x1 104 us: call_third(): pl.pallas_call(third_kernel, out_shape=[shape((count, model), BF16), shap...]
    all_gather x7 -> x0, waiting for transfers between devices: 245 us -> none  [the longest x1 72.8 us: on_device(): seq_grad = lax.all_gather(grad_out, 'blk', axis=0, tiled=True)]
    dot_general x24 -> x20, matrix products: 165 us -> 87.5 us  [the longest x6 34.9 us: dot_nt(): lax.dot_general(left, right, (((1,), (1,)), ((), ())), preferred_element_...]
    psum x1 -> x0, blocking collectives: 65.8 us -> none  [on_device(): gain_sums = lax.psum((grad_gain_rec, grad_gain_mlp), ('blk', 'tok'))]
    broadcast_in_dim x24 -> x0, other arithmetic: 36.9 us -> none  [the longest x14 18.3 us: linear_scan(): running = rates[:, step] * running + drives[:, step]]
    unnamed x384 -> x73, local copies, waits for them, and re-layouts: 43.3 us -> 14.9 us
  transfers between devices with their start and end apart: 18 -> 0, of which waited for: 13 -> 0; matrix products, arithmetic and copies ran while one was open for 37% -> 0% of each run, Pallas kernels for 0% -> 0%
where the time goes in v1:
time: 481 us; the launch traced here: 473 us
  Pallas kernels  330 us (69%)
  matrix products  87.5 us (18%)
  local copies, waits for them, and re-layouts  27 us (6%)
  blocking collectives  21.7 us (5%)
  other arithmetic  5.39 us (1%)
    pallas_call x1, Pallas kernels, call_third(): pl.pallas_call(third_kernel, out_shape=[shape((count, model), BF16), shap...  104 us
    pallas_call x1, Pallas kernels, call_middle(): pl.pallas_call(functools.partial(middle_kernel, widths, skip), out_shape=...  76.6 us
    pallas_call x1, Pallas kernels, call_fourth(): pl.pallas_call(fourth_kernel, out_shape=[shape((count, model), F32), fina...  60.4 us
    pallas_call x1, Pallas kernels, call_first(): pl.pallas_call(functools.partial(first_kernel, widths), out_shape=[shape(...  40 us
    dot_general x6, matrix products, dot_nt(): lax.dot_general(left, right, (((1,), (1,)), ((), ())), preferred_element_...  34.9 us
    dot_general x8, matrix products, dot_tn(): lax.dot_general(left, right, (((0,), (0,)), ((), ())), preferred_element_...  29.4 us
    pallas_call x1, Pallas kernels, recurrence_backward(): pl.pallas_call(functools.partial(backward_kernel, z_size), out_shape=[low...  25.7 us
    pallas_call x1, Pallas kernels, recurrence_forward(): pl.pallas_call(functools.partial(forward_kernel, z_size), out_shape=[jax....  23.2 us

profile of v1, /device:TPU:1, one launch (start us, length us, event | category | flops | bytes accessed | tf_op | source)
XLA Modules:
  0.0 473.2 jit_solution(16086315063664206659)
XLA Ops:
  2.5 11.3 %all-gather.1 = f32[32,160]{1,0:T(8,128)S(1)} all-gather(f32[8,160]{1,0:T(8,128)S(1)} %concatenate.22), channel_id=3, replica_groups=mesh['z'=4,'y'=4,'x'=4,'core'=2] {'z'}, dimensions={0}, use_global_device_ids=true | all-gather | bytes 25600 | tf_op jit(solution)/shard_map/all_gather | solution.py:1041
  18.6 10.4 %all-gather = bf16[8,160,160]{2,1,0:T(8,128)(2,1)S(1)} all-gather(bf16[2,160,160]{2,1,0:T(8,128)(2,1)S(1)} %pad_maximum_fusion), channel_id=2, replica_groups=mesh['z'=4,'y'=4,'x'=4,'core'=2] {'z'}, dimensions={0}, use_global_device_ids=true | all-gather | bytes 512000 | tf_op jit(solution)/shard_map/all_gather | solution.py:1045
  35.4 40.0 %shard_map.305 = (bf16[4,128,2048]{2,1,0:T(8,128)(2,1)}, bf16[4,160,2048]{2,1,0:T(8,128)(2,1)}, bf16[4,160,2048]{2,1,0:T(8,128)(2,1)}, bf16[4,160,2048]{2,1,0:T(8,128)(2,1)}) custom-call(bf16[128,2048]{1,0:T(8,128)(2,1)} %bitcast.101, f32[1,2048]{1,0:T(1,128)} %bitcast.132, bf16[1632,256]{1,0:T(8,128)(2,1)} %bitcast.104), custom_call_target="tpu_custom_call" | custom-call | tf_op jit(solution)/shard_map/pallas_call | solution.py:844
  75.4 5.4 %fusion.32.gelu_in = f32[512,640]{1,0:T(8,128)} fusion(bf16[512,2048]{1,0:T(8,128)(2,1)} %bitcast.159, bf16[640,2048]{1,0:T(8,128)(2,1)} %bitcast.153), kind=kOutput, calls=%fused_computation.72 | convolution fusion | flops 1342177280 | bytes 6029312 | tf_op jit(solution)/shard_map/dot_general | solution.py:26
  83.7 23.2 %shard_map.306 = (f32[520,640]{1,0:T(8,128)}, f32[512,640]{1,0:T(8,128)S(1)}, f32[512,640]{1,0:T(8,128)S(1)}, f32[512,640]{1,0:T(8,128)}, f32[512,640]{1,0:T(8,1...) custom-call(f32[512,640]{1,0:T(8,128)} %fusion.31.branch_in, f32[512,640]{1,0:T(8,128)} %fusion.32.gelu_in, ...), custom_call_target="tpu_custom_call" | custom-call | tf_op jit(solution)/shard_map/pallas_call | solution.py:940
  107.0 3.1 convolution_convert_fusion.7
  110.1 76.6 %shard_map.307 = (f32[128,2048]{1,0:T(8,128)}, bf16[4,128,2048]{2,1,0:T(8,128)(2,1)}, bf16[4,128,2048]{2,1,0:T(8,128)(2,1)}, bf16[4,384,2048]{2,1,0:T(8,128)(2,1...) custom-call(bf16[4,128,2048]{2,1,0:T(8,128)(2,1)} %bitcast.113, bf16[128,2048]{1,0:T(8,128)(2,1)} %bitcast.102, ...), custom_call_target="tpu_custom_call" | custom-call | tf_op jit(solution)/shard_map/pallas_call | solution.py:857
  186.7 8.7 %fusion.33 = f32[512,1536]{1,0:T(8,128)} fusion(bf16[512,2048]{1,0:T(8,128)(2,1)} %bitcast.165, bf16[1536,2048]{1,0:T(8,128)(2,1)} %bitcast.147), kind=kOutput, calls=%fused_computation.73 | convolution fusion | flops 3221225472 | bytes 11534336 | tf_op jit(solution)/shard_map/dot_general | solution.py:26
  195.4 5.1 %fusion.34 = f32[512,1536]{1,0:T(8,128)} fusion(bf16[512,2048]{1,0:T(8,128)(2,1)S(1)} %bitcast.166, bf16[1536,2048]{1,0:T(8,128)(2,1)S(1)} %bitcast.145), kind=kOutput, calls=%fused_computation.74 | convolution fusion | flops 3221225472 | bytes 11534336 | tf_op jit(solution)/shard_map/dot_general | solution.py:26
  200.5 8.3 %multiply_convert_fusion = (bf16[512,1536]{1,0:T(8,128)(2,1)S(1)}, bf16[512,1536]{1,0:T(8,128)(2,1)S(1)}, bf16[512,1536]{1,0:T(8,128)(2,1)S(1)}) fusion(f32[512,1536]{1,0:T(8,128)} %fusion.33, f32[512,1536]{1,0:T(8,128)} %fusion.34, bf16[512,2048]{1,0:T(8,128)(2,1)} %bitcast.169, bf16[1536,2048]{1,0:T(8,128)(2,1)S(1)} %bitcast.151), kind=kOutput, calls=%fused_computation.18 | convolution fusion | flops 3240886272 | bytes 19398656 | tf_op jit(solution)/shard_map/dot_general | solution.py:26
  208.8 5.0 %convolution_convert_fusion.6 = bf16[512,2048]{1,0:T(8,128)(2,1)} fusion(bf16[512,1536]{1,0:T(8,128)(2,1)S(1)} %get-tuple-element.146, bf16[1536,2048]{1,0:T(8,128)(2,1)S(1)} %bitcast.152), kind=kOutput, calls=%fused_computation.20 | convolution fusion | flops 3222274048 | bytes 9961472 | tf_op jit(solution)/shard_map/dot_general | solution.py:22
  213.9 3.4 fusion.35
  217.3 4.7 add_convert_fusion.1
  222.0 5.4 %convolution_convert_fusion = bf16[1536,2048]{1,0:T(8,128)(2,1)} fusion(bf16[512,1536]{1,0:T(8,128)(2,1)S(1)} %get-tuple-element.146, bf16[512,2048]{1,0:T(8,128)(2,1)S(1)} %bitcast.170), kind=kOutput, calls=%fused_computation | convolution fusion | flops 3224371200 | bytes 9961472 | tf_op jit(solution)/shard_map/dot_general | solution.py:30
  227.4 5.4 %convolution_convert_fusion.1 = bf16[1536,2048]{1,0:T(8,128)(2,1)} fusion(bf16[512,1536]{1,0:T(8,128)(2,1)S(1)} %get-tuple-element.144, bf16[512,2048]{1,0:T(8,128)(2,1)S(1)} %bitcast.167), kind=kOutput, calls=%fused_computation.1 | convolution fusion | flops 3224371200 | bytes 9961472 | tf_op jit(solution)/shard_map/dot_general | solution.py:30
  232.8 5.4 %convolution_convert_fusion.2 = bf16[1536,2048]{1,0:T(8,128)(2,1)} fusion(bf16[512,1536]{1,0:T(8,128)(2,1)S(1)} %get-tuple-element.145, bf16[512,2048]{1,0:T(8,128)(2,1)S(1)} %bitcast.168), kind=kOutput, calls=%fused_computation.2 | convolution fusion | flops 3224371200 | bytes 9961472 | tf_op jit(solution)/shard_map/dot_general | solution.py:30
  238.2 104.4 %shard_map.308 = (bf16[128,2048]{1,0:T(8,128)(2,1)}, f32[128,2048]{1,0:T(8,128)}, bf16[4,128,2048]{2,1,0:T(8,128)(2,1)}, f32[384,256]{1,0:T(8,128)}, f32[384,256...) custom-call(bf16[4,128,2048]{2,1,0:T(8,128)(2,1)} %bitcast.114, bf16[4,128,2048]{2,1,0:T(8,128)(2,1)} %bitcast.115, ...), custom_call_target="tpu_custom_call" | custom-call | tf_op jit(solution)/shard_map/pallas_call | solution.py:877
  342.6 4.5 fusion.36.g_gated
  347.1 25.7 %shard_map.309 = (bf16[512,640]{1,0:T(8,128)(2,1)S(1)}, bf16[512,640]{1,0:T(8,128)(2,1)S(1)}, bf16[512,640]{1,0:T(8,128)(2,1)S(1)}, bf16[512,640]{1,0:T(8,128)(2...) custom-call(f32[512,640]{1,0:T(8,128)} %fusion.36.g_gated, f32[512,640]{1,0:T(8,128)} %fusion.32.gelu_in, ...), custom_call_target="tpu_custom_call" | custom-call | tf_op jit(solution)/shard_map/pallas_call | solution.py:973
  387.3 3.7 fusion.37
  391.0 3.2 add_convert_fusion
  397.4 3.1 convolution_convert_fusion.5
  400.5 60.4 %shard_map.310 = (f32[128,2048]{1,0:T(8,128)}, f32[160,256]{1,0:T(8,128)}, f32[160,256]{1,0:T(8,128)}, f32[160,256]{1,0:T(8,128)}, f32[208,256]{1,0:T(8,128)}, /*index=5*/f32[8,2048]{1,0:T(8,128)}) custom-call(bf16[4,128,2048]{2,1,0:T(8,128)(2,1)} %bitcast.110, bf16[4,160,2048]{2,1,0:T(8,128)(2,1)} %bitcast.108, bf16[4,160,2048]{2,1,0:T(8,128)(2,1)} %bitcast.107, ...), custom_call_target="tpu_custom_call" | custom-call | tf_op jit(solution)/shard_map/pallas_call | solution.py:909
  460.9 3.4 copy.64
  (129 shorter events, 42.1 us)
Async XLA Ops:
  0.7 28.4 %copy-start.14 = (bf16[256,160]{0,1:T(8,128)(2,1)S(1)}, bf16[256,160]{0,1:T(8,128)(2,1)}, u32[]{:S(2)}) copy-start(bf16[256,160]{0,1:T(8,128)(2,1)} %param.30) | copy-start | bytes 245764
  0.7 28.3 %copy-start.13 = (bf16[256,160]{0,1:T(8,128)(2,1)S(1)}, bf16[256,160]{0,1:T(8,128)(2,1)}, u32[]{:S(2)}) copy-start(bf16[256,160]{0,1:T(8,128)(2,1)} %param.22) | copy-start | bytes 245764
  0.7 28.3 %copy-start.12 = (bf16[256,160]{0,1:T(8,128)(2,1)S(1)}, bf16[256,160]{0,1:T(8,128)(2,1)}, u32[]{:S(2)}) copy-start(bf16[256,160]{0,1:T(8,128)(2,1)} %param.21) | copy-start | bytes 245764
  75.4 5.4 %copy-start.18 = (bf16[4,160,2048]{2,1,0:T(8,128)(2,1)S(1)}, bf16[4,160,2048]{2,1,0:T(8,128)(2,1)}, u32[]{:S(2)}) copy-start(bf16[4,160,2048]{2,1,0:T(8,128)(2,1)} %get-tuple-element.54) | copy-start | bytes 7864324
  75.4 5.4 %copy-start.21 = (bf16[4,128,2048]{2,1,0:T(8,128)(2,1)S(1)}, bf16[4,128,2048]{2,1,0:T(8,128)(2,1)}, u32[]{:S(2)}) copy-start(bf16[4,128,2048]{2,1,0:T(8,128)(2,1)} %get-tuple-element.53) | copy-start | bytes 6291460
  83.7 23.2 %copy-start.19 = (bf16[4,160,2048]{2,1,0:T(8,128)(2,1)S(1)}, bf16[4,160,2048]{2,1,0:T(8,128)(2,1)}, u32[]{:S(2)}) copy-start(bf16[4,160,2048]{2,1,0:T(8,128)(2,1)} %get-tuple-element.57) | copy-start | bytes 7864324
  107.0 3.1 copy-start
  107.0 3.1 copy-start.1
  186.7 8.7 %copy-start.15 = (bf16[4,384,2048]{2,1,0:T(8,128)(2,1)S(1)}, bf16[4,384,2048]{2,1,0:T(8,128)(2,1)}, u32[]{:S(2)}) copy-start(bf16[4,384,2048]{2,1,0:T(8,128)(2,1)} %get-tuple-element.60) | copy-start | bytes 18874372
  186.7 8.7 %copy-start.24 = (bf16[4,128,2048]{2,1,0:T(8,128)(2,1)S(1)}, bf16[4,128,2048]{2,1,0:T(8,128)(2,1)}, u32[]{:S(2)}) copy-start(bf16[4,128,2048]{2,1,0:T(8,128)(2,1)} %get-tuple-element.58) | copy-start | bytes 6291460
  195.4 5.1 %copy-start.16 = (bf16[4,384,2048]{2,1,0:T(8,128)(2,1)S(1)}, bf16[4,384,2048]{2,1,0:T(8,128)(2,1)}, u32[]{:S(2)}) copy-start(bf16[4,384,2048]{2,1,0:T(8,128)(2,1)} %get-tuple-element.61) | copy-start | bytes 18874372
  195.4 18.5 %slice-start = ((s8[6291456]{0:T(1024)(128)(4,1)}), s8[4194304]{0:T(1024)(128)(4,1)S(1)}, s32[]{:S(2)}) async-start(s8[6291456]{0:T(1024)(128)(4,1)} %bitcast.148), calls=%async_computation | async-start | bytes 8388608
  200.5 13.3 %slice-start.1 = ((s8[6291456]{0:T(1024)(128)(4,1)}), s8[2097152]{0:T(1024)(128)(4,1)S(1)}, s32[]{:S(2)}) async-start(s8[6291456]{0:T(1024)(128)(4,1)} %bitcast.148), calls=%async_computation.1 | async-start | bytes 4194304
  217.3 4.7 copy-start.25
  238.2 104.4 %copy-start.20 = (bf16[4,160,2048]{2,1,0:T(8,128)(2,1)S(1)}, bf16[4,160,2048]{2,1,0:T(8,128)(2,1)}, u32[]{:S(2)}) copy-start(bf16[4,160,2048]{2,1,0:T(8,128)(2,1)} %get-tuple-element.57) | copy-start | bytes 7864324
  347.1 25.7 %copy-start.23 = (bf16[4,128,2048]{2,1,0:T(8,128)(2,1)S(1)}, bf16[4,128,2048]{2,1,0:T(8,128)(2,1)}, u32[]{:S(2)}) copy-start(bf16[4,128,2048]{2,1,0:T(8,128)(2,1)} %get-tuple-element.65) | copy-start | bytes 6291460
  380.3 5.1 %copy-start.8 = (f32[384,256]{1,0:T(8,128)S(1)}, f32[384,256]{1,0:T(8,128)}, u32[]{:S(2)}) copy-start(f32[384,256]{1,0:T(8,128)} %get-tuple-element.87) | copy-start | bytes 1179652
  380.5 5.9 %copy-start.7 = (f32[384,256]{1,0:T(8,128)S(1)}, f32[384,256]{1,0:T(8,128)}, u32[]{:S(2)}) copy-start(f32[384,256]{1,0:T(8,128)} %get-tuple-element.88) | copy-start | bytes 1179652
  387.3 3.7 copy-start.17
  391.0 3.2 copy-start.22
  460.8 9.4 %copy-start.6 = (bf16[128,2048]{1,0:T(8,128)(2,1)S(1)}, bf16[128,2048]{1,0:T(8,128)(2,1)}, u32[]{:S(2)}) copy-start(bf16[128,2048]{1,0:T(8,128)(2,1)} %get-tuple-element.64) | copy-start | bytes 1572868
  460.8 10.2 %copy-start.11 = (f32[160,256]{1,0:T(8,128)S(1)}, f32[160,256]{1,0:T(8,128)}, u32[]{:S(2)}) copy-start(f32[160,256]{1,0:T(8,128)} %get-tuple-element.82) | copy-start | bytes 491524
  460.9 10.9 %copy-start.10 = (f32[160,256]{1,0:T(8,128)S(1)}, f32[160,256]{1,0:T(8,128)}, u32[]{:S(2)}) copy-start(f32[160,256]{1,0:T(8,128)} %get-tuple-element.83) | copy-start | bytes 491524
  460.9 11.5 %copy-start.9 = (f32[160,256]{1,0:T(8,128)S(1)}, f32[160,256]{1,0:T(8,128)}, u32[]{:S(2)}) copy-start(f32[160,256]{1,0:T(8,128)} %get-tuple-element.85) | copy-start | bytes 491524
  (4 other events, 10.2 us)
